TPU v7x, 256 devices: a whole 4x4x8 slice. The times are simulated.
256 devices in a mesh: pool: 32 (over x, z_lo, y), tensor: 8 (over z_hi, core).
Axes of the slice: x: 4, y: 4, z: 8 (z_hi: 4, z_lo: 2; z = z_hi * 2 + z_lo), core: 2. Of those that a mesh axis runs over, the one named last changes fastest.
Arguments:
- queries: bfloat16 [16384, 4096], P('pool', 'tensor'), may hold values from -400 to 400
- new_key_value: bfloat16 [16384, 2, 1024], P('pool', None, 'tensor'), may hold values from -5 to 5
- saved_key_value: bfloat16 [1024, 128, 2, 1024], P('pool', None, None, 'tensor'), may hold values from -5 to 5
- out_weight: bfloat16 [4096, 5120], P('tensor'), may hold values from -5 to 5
- hist_owner: int32 [32, 64], P('pool'), may hold values from 0 to 31, as said below
- hist_block: int32 [32, 64], P('pool'), may hold values from 0 to 31
- hist_len: int32 [32], P('pool'), may hold values from 8 to 64, as said below
- evict: int32 [32], P('pool'), may hold values 0 or 1
- dest_owner: int32 [32, 4], P('pool'), may hold values from 0 to 31, as said below
- dest_slot: int32 [32, 4], P('pool'), may hold values from 0 to 31, as said below
Outputs:
- attn_out: bfloat16 [16384, 5120], P(('pool', 'tensor'))
- pool_out: bfloat16 [1024, 128, 2, 1024], P('pool', None, None, 'tensor')
Inputs may be any that keep to these rules, and one draw needn't show every extreme that they name: `hist_owner`: in row p each owner appears exactly 2 times among all 64 entries, so at most 2 times among the first hist_len[p]. `hist_len`: some instance has all 64 blocks. `dest_owner`: the 4 owners of one row are distinct, and each column names every owner once. All pairs (dest_owner, dest_slot) are distinct.
All inputs are finite; a program needn't handle non-finite values. No bound on the sum of `evict` on one device may be relied on, other than what follows from the above.
Results may differ from a plain program's by a relative error of at most 0.017.
Values may be sent and summed in bfloat16 or wider, within the bound.
No kernel may reach another device: no remote copies, remote signals or barrier semaphores. Data moves between devices by JAX's collectives and lax.ppermute only.
A program may use at most 128 MiB of HBM per device.

v0:
```python
import functools
import math

import jax
import jax.numpy as jnp
from jax import lax
from jax.experimental import pallas as pl
from jax.experimental.pallas import tpu as pltpu
from jax.sharding import PartitionSpec as P

HEAD = 128
CHUNK = 8
PART = 32
NT = (((1,), (1,)), ((), ()))
SMEM = pl.BlockSpec(memory_space=pltpu.SMEM)
VMEM = pl.BlockSpec(memory_space=pltpu.VMEM)
ANY = pl.BlockSpec(memory_space=pl.ANY)
HBM = pl.BlockSpec(memory_space=pltpu.HBM)


def limit(mebibytes):
    return pltpu.CompilerParams(vmem_limit_bytes=mebibytes * 2**20)


def table_kernel(
    length, dest_owner, dest_slot, evict, owner_ref, block_ref, new_ref, table_ref, list_ref, rows_ref
):
    pool, entries = table_ref.shape[0], owner_ref.shape[1]
    owner = jnp.broadcast_to(owner_ref[...], (pool, entries))
    block = jnp.broadcast_to(block_ref[...], (pool, entries))
    row = lax.broadcasted_iota(jnp.int32, (pool, entries), 0)
    col = lax.broadcasted_iota(jnp.int32, (pool, entries), 1)
    match = owner == row
    first = jnp.min(jnp.where(match, col, entries), axis=1, keepdims=True)
    second = jnp.max(jnp.where(match, col, -1), axis=1, keepdims=True)
    want0 = jnp.sum(jnp.where(match & (col == first), block, 0), axis=1, keepdims=True)
    want1 = jnp.sum(jnp.where(match & (col == second), block, 0), axis=1, keepdims=True)
    row = lax.broadcasted_iota(jnp.int32, (pool, 128), 0)
    lane = lax.broadcasted_iota(jnp.int32, (pool, 128), 1)
    used0 = jnp.where(jnp.broadcast_to(first, (pool, 128)) < length[0], 1, 0)
    used1 = jnp.where(jnp.broadcast_to(second, (pool, 128)) < length[0], 1, 0)
    used = (used0 + used1).astype(jnp.float32)
    earlier = jnp.where(
        lax.broadcasted_iota(jnp.int32, (pool, pool), 1)
        < lax.broadcasted_iota(jnp.int32, (pool, pool), 0),
        1.0,
        0.0,
    )
    before = jnp.dot(earlier, used, preferred_element_type=jnp.float32).astype(jnp.int32)
    place = jnp.where((used0 > 0) & (before == lane), 2 * row, 0)
    place += jnp.where((used1 > 0) & (before + used0 == lane), 2 * row + 1, 0)
    quarter = pool // 4
    counts = jnp.where(row < quarter * (lane + 1), used0 + used1, 0)
    list_ref[...] = jnp.zeros(list_ref.shape, jnp.int32)
    list_ref[0:1] = jnp.sum(place, axis=0, keepdims=True)
    list_ref[1:2] = jnp.sum(counts, axis=0, keepdims=True)

    out = jnp.where(lane == 0, want0, jnp.where(lane == 1, want1, 0))
    for b in range(4):
        out = jnp.where(lane == 2 + b, dest_owner[0, b], out)
        out = jnp.where(lane == 6 + b, dest_slot[0, b], out)
    out = jnp.where(lane == 10, evict[0], out).astype(jnp.float32)
    for b in range(4):
        fresh = new_ref[b].astype(jnp.float32)
        for o in range(pool):
            rows_ref[o, 8 * b : 8 * b + 8, :] = fresh[8 * o : 8 * o + 8]
    for o in range(pool):
        rows_ref[o, 32:48, :] = jnp.broadcast_to(out[o : o + 1], (16, 128))
    table_ref[...] = rows_ref[...].astype(jnp.bfloat16)


def exchange_table(hist_owner, hist_block, hist_len, dest_owner, dest_slot, evict, new_blocks, pool):
    return pl.pallas_call(
        table_kernel,
        out_shape=(
            jax.ShapeDtypeStruct((pool, 48, 128), jnp.bfloat16),
            jax.ShapeDtypeStruct((8, 128), jnp.int32),
        ),
        in_specs=[SMEM, SMEM, SMEM, SMEM, VMEM, VMEM, VMEM],
        out_specs=(VMEM, VMEM),
        scratch_shapes=[pltpu.VMEM((pool, 48, 128), jnp.float32)],
        compiler_params=limit(58),
        name="table",
    )(hist_len, dest_owner, dest_slot, evict, hist_owner, hist_block, new_blocks)


def split_kernel(x_ref, o_ref):
    row = lax.broadcasted_iota(jnp.int32, (128, 256), 0)
    source = lax.broadcasted_iota(jnp.int32, (128, 256), 1)
    pick_k = jnp.where(source == 2 * row, 1.0, 0.0).astype(jnp.bfloat16)
    pick_v = jnp.where(source == 2 * row + 1, 1.0, 0.0).astype(jnp.bfloat16)
    for b in range(x_ref.shape[0]):
        x = x_ref[b]
        k = jnp.dot(pick_k, x, preferred_element_type=jnp.float32)
        v = jnp.dot(pick_v, x, preferred_element_type=jnp.float32)
        o_ref[b, 0:128, :] = k.astype(jnp.bfloat16)
        o_ref[b, 128:256, :] = v.T.astype(jnp.bfloat16)


def split_blocks(x):
    return pl.pallas_call(
        split_kernel,
        out_shape=jax.ShapeDtypeStruct(x.shape, x.dtype),
        in_specs=[VMEM],
        out_specs=VMEM,
        compiler_params=limit(12),
        name=f"split{x.shape[0]}",
    )(x)


def gather_kernel(told, pool_ref, held_ref, out_ref, held, onward, packed, sems):
    pool, rows = packed.shape[:2]
    copies = []
    for p in range(pool):
        for r in range(2):
            copies.append(
                pltpu.make_async_copy(
                    pool_ref.at[told[p, r]], out_ref.at[p, pl.ds(256 * r, 256)], sems.at[2 * p + r]
                )
            )
            copies[-1].start()
    held[...] = held_ref[...].astype(jnp.float32)
    for b in range(4):
        for p in range(pool):
            onward[told[p, 2 + b], 8 * b : 8 * b + 8, :] = held[p, 8 * b : 8 * b + 8, :]
    packed[...] = onward[...].astype(jnp.bfloat16)
    copies.append(
        pltpu.make_async_copy(packed, out_ref.at[:, pl.ds(512, rows)], sems.at[2 * pool])
    )
    copies[-1].start()
    for copy in copies:
        copy.wait()


def gather_blocks(told, pool_blocks, held):
    pool, rows, _ = held.shape
    return pl.pallas_call(
        gather_kernel,
        out_shape=jax.ShapeDtypeStruct((pool, 512 + rows, 128), pool_blocks.dtype),
        in_specs=[SMEM, VMEM, VMEM],
        out_specs=HBM,
        scratch_shapes=[
            pltpu.VMEM(held.shape, jnp.float32),
            pltpu.VMEM(held.shape, jnp.float32),
            pltpu.VMEM(held.shape, jnp.bfloat16),
            pltpu.SemaphoreType.DMA((2 * pool + 1,)),
        ],
        compiler_params=limit(51),
        name="gather",
    )(told, pool_blocks, held)


def accumulate(state, s, vt):
    m, l, acc = state
    c = math.log2(math.e) / math.sqrt(HEAD)
    top = jnp.maximum(m, jnp.max(s, axis=0, keepdims=True))
    p = jnp.exp2(s * c - top * c)
    keep = jnp.exp2((m - top) * c)
    l = l * keep + jnp.sum(p, axis=0, keepdims=True)
    acc = acc * keep + jnp.dot(vt, p.astype(jnp.bfloat16), preferred_element_type=jnp.float32)
    return top, l, acc


def begin_kernel(base, q_ref, new_ref, *refs):
    c = math.log2(math.e) / math.sqrt(HEAD)
    heads = q_ref.shape[1] // HEAD
    blocks = new_ref.shape[0]
    k = jnp.concatenate([new_ref[i, 0:128, :] for i in range(blocks)], axis=0)
    vt = jnp.concatenate([new_ref[i, 128:256, :] for i in range(blocks)], axis=1)
    before = 0
    for group in range(len(refs) // 4):
        out_q, out_m, out_l, out_acc = refs[4 * group : 4 * group + 4]
        rows = out_q.shape[0]
        tok = rows // heads
        parts = tok // PART
        key = lax.broadcasted_iota(jnp.int32, (blocks * 128, rows), 0)
        at = lax.broadcasted_iota(jnp.int32, (1, rows), 1) & (tok - 1)
        token = base[before] + at
        for i in range(1, parts):
            token = jnp.where(at >= PART * i, base[before + i] + at - PART * i, token)
        for i in range(parts):
            first = pl.multiple_of(base[before + i], PART)
            for h in range(heads):
                out_q[pl.ds(h * tok + i * PART, PART), :] = q_ref[
                    pl.ds(first, PART), h * HEAD : (h + 1) * HEAD
                ]
        s = lax.dot_general(k, out_q[...], NT, preferred_element_type=jnp.float32)
        s = jnp.where(key <= token, s, -jnp.inf)
        m = jnp.max(s, axis=0, keepdims=True)
        p = jnp.exp2(s * c - m * c)
        out_m[...] = m
        out_l[...] = jnp.sum(p, axis=0, keepdims=True)
        out_acc[...] = jnp.dot(vt, p.astype(jnp.bfloat16), preferred_element_type=jnp.float32)
        before += parts


def begin(queries, fresh, base, sizes):
    out_shape = ()
    for parts in sizes:
        rows = parts * PART * queries.shape[1] // HEAD
        out_shape += (
            jax.ShapeDtypeStruct((rows, HEAD), queries.dtype),
            jax.ShapeDtypeStruct((1, rows), jnp.float32),
            jax.ShapeDtypeStruct((1, rows), jnp.float32),
            jax.ShapeDtypeStruct((HEAD, rows), jnp.float32),
        )
    out = pl.pallas_call(
        begin_kernel,
        out_shape=out_shape,
        in_specs=[SMEM, VMEM, VMEM],
        out_specs=(VMEM,) * len(out_shape),
        compiler_params=limit(24),
        name="begin",
    )(base, queries, fresh)
    return [out[4 * g : 4 * g + 4] for g in range(len(sizes))]


def attend_kernel(
    blocks, length, q_ref, m_ref, l_ref, acc_ref, kv_any, mine_ref, theirs_ref, sbuf, kv_ref, sems
):
    quarters = sems.shape[0]
    share = kv_ref.shape[0] // quarters

    def quarter(k):
        owners = pl.ds(pl.multiple_of(k * share, share), share)
        return pltpu.make_async_copy(
            kv_any.at[owners, pl.ds(0, kv_ref.shape[1])], kv_ref.at[owners], sems.at[k]
        )

    def wait(k, _):
        quarter(k).wait()
        return 0

    for k in range(quarters):
        quarter(k).start()
    rows = q_ref.shape[0]
    tok = mine_ref.shape[0] * 2
    heads = rows // tok
    q = q_ref[...]

    def half(i, u, value):
        place = blocks[0, i * CHUNK + u]
        start = pl.multiple_of((place % 2) * 256 + 128 * value, 128)
        return kv_ref[place // 2, pl.ds(start, 128), :]

    def values_of(i):
        return jnp.concatenate([half(i, u, 1) for u in range(CHUNK)], axis=1)

    def scores(i):
        keys = jnp.concatenate([half(i, u, 0) for u in range(CHUNK)], axis=0)
        return lax.dot_general(keys, q, NT, preferred_element_type=jnp.float32)

    n = length[0]
    full = n // CHUNK
    last = 2 * kv_ref.shape[0] // CHUNK - 1
    opening = sum(jnp.where(blocks[1, k] < CHUNK, 1, 0) for k in range(quarters - 1))
    lax.fori_loop(0, opening + 1, wait, 0)
    sbuf[0] = scores(0)

    def step(i, state, a):
        sbuf[1 - a] = scores(jnp.minimum(i + 1, last))
        return accumulate(state, sbuf[a], values_of(i))

    def two(i, state):
        return step(2 * i + 1, step(2 * i, state, 0), 1)

    def upto(k):
        some = jnp.maximum(blocks[1, k] // CHUNK - 1, 0) // 2
        return jnp.where(k == quarters - 1, full // 2, some)

    def part(k, state):
        lax.fori_loop(jnp.where(k == opening, k + 1, k), k + 1, wait, 0)
        start = jnp.where(k == opening, 0, upto(jnp.maximum(k - 1, 0)))
        return lax.fori_loop(start, upto(k), two, state)

    state = (m_ref[...], l_ref[...], acc_ref[...])
    state = lax.fori_loop(opening, quarters, part, state)
    state = lax.fori_loop(full // 2 * 2, full, lambda i, st: step(i, st, 0), state)

    def tail(i, state):
        position = i * (CHUNK * 128) + lax.broadcasted_iota(jnp.int32, (CHUNK * 128, rows), 0)
        s = jnp.where(position < n * 128, scores(i), -jnp.inf)
        return accumulate(state, s, values_of(i))

    m, l, acc = lax.fori_loop(full, (n + CHUNK - 1) // CHUNK, tail, state)
    context = (acc / l).T.astype(jnp.bfloat16)
    own = tok // 2
    for h in range(heads):
        mine_ref[:, h * HEAD : (h + 1) * HEAD] = context[h * tok : h * tok + own]
        theirs_ref[:, h * HEAD : (h + 1) * HEAD] = context[h * tok + own : (h + 1) * tok]


def attend(start, kv, blocks, length, heads, group):
    q, m, l, acc = start
    rows = q.shape[0]
    out = jax.ShapeDtypeStruct((rows // heads // 2, heads * HEAD), jnp.bfloat16)
    return pl.pallas_call(
        attend_kernel,
        out_shape=(out, out),
        in_specs=[SMEM, SMEM, VMEM, VMEM, VMEM, VMEM, HBM],
        out_specs=(VMEM, VMEM),
        scratch_shapes=[
            pltpu.VMEM((2, CHUNK * 128, rows), jnp.float32),
            pltpu.VMEM((kv.shape[0], 512, 128), kv.dtype),
            pltpu.SemaphoreType.DMA((4,)),
        ],
        compiler_params=limit(50),
        name=f"attend{group}",
    )(blocks, length, q, m, l, acc, kv)


def project_kernel(a_ref, b_ref, *refs, arriving):
    arrived, (wa_any, wb_any) = refs[:arriving], refs[arriving : arriving + 2]
    outs, (wa_ref, wb_ref, sems) = refs[arriving + 2 : -3], refs[-3:]
    tiles = sems.shape[0]
    tile = wa_ref.shape[1] // tiles
    copies = []
    for j in range(tiles):
        cols = pl.ds(j * tile, tile)
        copies.append(
            (
                pltpu.make_async_copy(wa_any.at[:, cols], wa_ref.at[:, cols], sems.at[j, 0]),
                pltpu.make_async_copy(wb_any.at[:, cols], wb_ref.at[:, cols], sems.at[j, 1]),
            )
        )
        for copy in copies[-1]:
            copy.start()
    for j in range(tiles):
        cols = slice(j * tile, (j + 1) * tile)
        for copy in copies[j]:
            copy.wait()
        total = jnp.dot(a_ref[...], wa_ref[:, cols], preferred_element_type=jnp.float32)
        total += jnp.dot(b_ref[...], wb_ref[:, cols], preferred_element_type=jnp.float32)
        for i, out_ref in enumerate(outs):
            one = total[i * PART : (i + 1) * PART]
            if arrived:
                one += arrived[i][:, cols].astype(jnp.float32)
            out_ref[:, cols] = one.astype(jnp.bfloat16)


def project(a, b, wa, wb, *arrived):
    out = jax.ShapeDtypeStruct((PART, wa.shape[1]), jnp.bfloat16)
    parts = a.shape[0] // PART
    return pl.pallas_call(
        functools.partial(project_kernel, arriving=len(arrived)),
        out_shape=(out,) * parts,
        in_specs=[VMEM] * (2 + len(arrived)) + [HBM, HBM],
        out_specs=(VMEM,) * parts,
        scratch_shapes=[
            pltpu.VMEM(wa.shape, wa.dtype),
            pltpu.VMEM(wb.shape, wb.dtype),
            pltpu.SemaphoreType.DMA((10, 2)),
        ],
        compiler_params=limit(50),
        name=f"project{parts}",
    )(a, b, *arrived, wa, wb)


def combine_kernel(top, bottom, far_up, near_down, near_up, far_down, o_ref):
    half = top.shape[0]
    for rows, parts in ((0, (top, far_up, near_down)), (half, (bottom, near_up, far_down))):
        total = sum(part[...].astype(jnp.float32) for part in parts)
        o_ref[rows : rows + half, :] = total.astype(jnp.bfloat16)


def combine(*parts):
    rows, width = parts[0].shape
    return pl.pallas_call(
        combine_kernel,
        out_shape=jax.ShapeDtypeStruct((2 * rows, width), jnp.bfloat16),
        in_specs=[VMEM] * 6,
        out_specs=VMEM,
        compiler_params=limit(8),
        name="combine",
    )(*parts)


def copy_kernel(x_ref, o_ref, buf, sem):
    for source, target in ((x_ref, buf), (buf, o_ref)):
        copy = pltpu.make_async_copy(source, target, sem)
        copy.start()
        copy.wait()


def copy_pool(x):
    return pl.pallas_call(
        copy_kernel,
        out_shape=jax.ShapeDtypeStruct(x.shape, x.dtype),
        in_specs=[HBM],
        out_specs=HBM,
        scratch_shapes=[pltpu.VMEM(x.shape, x.dtype), pltpu.SemaphoreType.DMA],
        compiler_params=limit(4),
        name="copy_pool",
    )(x)


def write_kernel(slots, fresh_ref, kept_ref, out_ref, sems):
    del kept_ref
    for b in range(fresh_ref.shape[0]):

        @pl.when(slots[b] >= 0)
        def _(b=b):
            copy = pltpu.make_async_copy(fresh_ref.at[b], out_ref.at[slots[b]], sems.at[b])
            copy.start()
            copy.wait()


def write_back(slots, fresh, kept):
    return pl.pallas_call(
        write_kernel,
        out_shape=jax.ShapeDtypeStruct(kept.shape, kept.dtype),
        in_specs=[SMEM, VMEM, ANY],
        out_specs=ANY,
        input_output_aliases={2: 0},
        scratch_shapes=[pltpu.SemaphoreType.DMA((fresh.shape[0],))],
        compiler_params=limit(4),
        name="write",
    )(slots, fresh, kept)


def swap_pool(x):
    return lax.all_to_all(x, "pool", split_axis=0, concat_axis=0, tiled=True)


def on_device(
    queries,
    new_key_value,
    saved,
    out_weight,
    hist_owner,
    hist_block,
    hist_len,
    evict,
    dest_owner,
    dest_slot,
):
    pool = lax.axis_size("pool")
    me = lax.axis_index("pool")
    chips = lax.axis_size("tensor") // 2
    chip, core = lax.axis_index("tensor") // 2, lax.axis_index("tensor") % 2
    other_core = [(2 * z + c, 2 * z + 1 - c) for z in range(chips) for c in range(2)]
    upward = [(2 * z + c, 2 * ((z + 1) % chips) + c) for z in range(chips) for c in range(2)]
    downward = [(target, source) for source, target in upward]
    swap = functools.partial(lax.ppermute, axis_name="tensor", perm=other_core)
    send_up = functools.partial(lax.ppermute, axis_name="tensor", perm=upward)
    send_down = functools.partial(lax.ppermute, axis_name="tensor", perm=downward)

    def part(offset, c, half):
        return 128 * ((chip + offset) % chips) + 64 * c + PART * half

    plan = (((2, 0), (2, 1), (1, 1), (3, 0)), ((1, 0), (3, 1)), ((0, 0), (0, 1)))
    base = jnp.stack(
        [part(o, c, h) for parts in plan for c in (core, 1 - core) for o, h in parts]
    ).astype(jnp.int32)

    new_blocks = new_key_value.reshape(-1, 256, 128)
    table, blocks = exchange_table(
        hist_owner, hist_block, hist_len, dest_owner, dest_slot, evict, new_blocks, pool
    )
    arrived = swap_pool(table)
    pool_blocks = split_blocks(saved.reshape(-1, 256, 128))
    told = arrived[:, 32, :].astype(jnp.int32)
    kv = swap_pool(gather_blocks(told, pool_blocks, arrived[:, :32]))
    starts = begin(
        queries, split_blocks(new_blocks), base, [2 * len(parts) for parts in plan]
    )
    other_weight = swap(out_weight)
    kept = copy_pool(saved.reshape(-1, 256, 128))

    heads = queries.shape[1] // HEAD

    def contexts(group, after):
        used, _ = lax.optimization_barrier((blocks, after))
        mine, theirs = attend(starts[group], kv, used, hist_len, heads, group)
        return mine, swap(theirs)

    up, down, near_up, near_down = project(
        *contexts(0, (kept, starts)), out_weight, other_weight
    )
    through_up, through_down = send_up(up), send_down(down)
    near_up, near_down = send_up(near_up), send_down(near_down)
    up, down = project(*contexts(1, up), out_weight, other_weight, through_up, through_down)
    far_up, far_down = send_up(up), send_down(down)

    returned = kv[:, 512:].reshape(pool, 4, 8, 128).transpose(1, 0, 2, 3)
    mine = (told[:, 2:6] == me) & (told[:, 10:11] > 0)
    slots = jnp.max(jnp.where(mine, told[:, 6:10], -1), axis=0)
    top, bottom = project(*contexts(2, up), out_weight, other_weight)
    returned, _ = lax.optimization_barrier((returned, top))
    pool_out = write_back(slots, returned.reshape(4, 256, 128), kept).reshape(saved.shape)
    attn_out = combine(top, bottom, far_up, near_down, near_up, far_down)
    return attn_out, pool_out


def solution(mesh):
    in_specs = (
        P("pool", "tensor"),
        P("pool", None, "tensor"),
        P("pool", None, None, "tensor"),
        P("tensor", None),
        P("pool", None),
        P("pool", None),
        P("pool"),
        P("pool"),
        P("pool", None),
        P("pool", None),
    )
    out_specs = (P(("pool", "tensor"), None), P("pool", None, None, "tensor"))
    return jax.shard_map(
        on_device, mesh=mesh, in_specs=in_specs, out_specs=out_specs, check_vma=False
    )
```

profile of v0, /device:TPU:13, one launch (start us, length us, event | category | flops | bytes accessed | tf_op | source)
XLA Modules:
  0.0 164.9 jit_solution(14573137435699456053)
XLA Ops:
  1.9 2.0 %table.1 = (bf16[32,48,128]{2,1,0:T(8,128)(2,1)}, s32[8,128]{1,0:T(8,128)}) custom-call(s32[1]{0:T(128)S(6)} %copy.17.length, s32[1,4]{1,0:T(1,128)} %dest_owner.1, s32[1,4]{1,0:T(1,128)} %dest_slot.1, s32[1]{0:T(128)S(6)} %copy.18.evict, s32[1,64]{1,0:T(1,128)} %owner_ref.1, s32[1,64]{1,0:T(1,128)} %block_ref.1, bf16[4,256,128]{2,1,0:T(8,128)(2,1)} %bitcast.29), custom_call_target="tpu_custom_call" | custom-call | tf_op jit(solution)/shard_map/table/pallas_call | solution.py:73
  3.9 8.3 %all-to-all-start = ((bf16[32,48,128]{2,1,0:T(8,128)(2,1)}), bf16[32,48,128]{2,1,0:T(8,128)(2,1)S(1)}, u32[]{:S(2)}, u32[]{:S(2)}) async-start(bf16[32,48,128]{2,1,0:T(8,128)(2,1)} %get-tuple-element.48), calls=%async_computation | async-start | bytes 786432 | tf_op jit(solution)/shard_map/all_to_all | solution.py:422
  12.2 0.0 copy-start
  12.2 1.6 copy-done
  13.8 1.3 split32.1.pool_ref
  15.1 3.9 %all-to-all-done = bf16[32,48,128]{2,1,0:T(8,128)(2,1)S(1)} async-done(((bf16[32,48,128]{2,1,0:T(8,128)(2,1)}), bf16[32,48,128]{2,1,0:T(8,128)(2,1)S(1)}, u32[]{:S(2)}, u32[]{:S(2)}) %all-to-all-start) | async-done | bytes 393248 | tf_op jit(solution)/shard_map/all_to_all | solution.py:422
  19.1 3.5 %gather.1 = bf16[32,544,128]{2,1,0:T(8,128)(2,1)} custom-call(s32[32,128]{1,0:T(8,128)S(1)} %bitcast.31, bf16[32,256,128]{2,1,0:T(8,128)(2,1)S(1)} %split32.1.pool_ref, bf16[32,32,128]{2,1,0:T(8,128)(2,1)S(1)} %slice.25.held_ref), custom_call_target="tpu_custom_call" | custom-call | tf_op jit(solution)/shard_map/gather/pallas_call | solution.py:137
  22.6 0.0 copy-start.1
  22.6 0.0 copy-start.2
  22.6 6.8 %all-to-all-start.1 = ((bf16[32,544,128]{2,1,0:T(8,128)(2,1)}), bf16[32,544,128]{2,1,0:T(8,128)(2,1)}, u32[]{:S(2)}, u32[]{:S(2)}) async-start(bf16[32,544,128]{2,1,0:T(8,128)(2,1)} %gather.1), calls=%async_computation.1 | async-start | bytes 8912896 | tf_op jit(solution)/shard_map/all_to_all | solution.py:422
  29.4 0.0 copy-start.3
  29.5 0.0 copy-start.4
  29.5 3.0 %collective-permute-start.1 = (bf16[512,5120]{1,0:T(8,128)(2,1)}, bf16[512,5120]{1,0:T(8,128)(2,1)}, u32[]{:S(2)}, u32[]{:S(2)}) collective-permute-start(bf16[512,5120]{1,0:T(8,128)(2,1)} %refs_0_.3), channel_id=1, source_target_pairs={{0,1},{1,0},{2,3},{3,2},{4,5},{5,4},{6,7},{7,6},{8,9},{9,8},{10,11... | collective-permute-start | bytes 15728648 | tf_op jit(solution)/shard_map/ppermute | solution.py:467
  32.4 0.0 copy-done.1
  32.4 1.5 copy_pool.1.kept_ref
  34.0 0.0 copy-done.2
  34.0 0.3 split4.1.new_ref
  34.4 0.1 stack.67.base
  34.5 0.0 copy-done.3
  34.5 2.8 %begin.1 = (bf16[1024,128]{1,0:T(8,128)(2,1)S(1)}, f32[1,1024]{1,0:T(1,128)S(1)}, f32[1,1024]{1,0:T(1,128)S(1)}, f32[128,1024]{1,0:T(8,128)S(1)}, bf16[512,128]{...) custom-call(s32[16]{0:T(128)S(1)} %stack.67.base, ...), custom_call_target="tpu_custom_call" | custom-call | tf_op jit(solution)/shard_map/begin/pallas_call | solution.py:207
  37.3 47.1 %all-to-all-done.1.kv_any = bf16[32,544,128]{2,1,0:T(8,128)(2,1)} async-done(((bf16[32,544,128]{2,1,0:T(8,128)(2,1)}), bf16[32,544,128]{2,1,0:T(8,128)(2,1)}, u32[]{:S(2)}, u32[]{:S(2)}) %all-to-all-start.1) | async-done | bytes 4456480 | tf_op jit(solution)/shard_map/all_to_all | solution.py:422
  84.4 0.0 copy-done.4
  84.4 15.4 %attend0.1 = (bf16[128,512]{1,0:T(8,128)(2,1)S(1)}, bf16[128,512]{1,0:T(8,128)(2,1)S(1)}) custom-call(s32[8,128]{1,0:T(8,128)S(1)} %copy-done.4, s32[1]{0:T(128)S(6)} %copy.17.length, bf16[1024,128]{1,0:T(8,128)(2,1)S(1)} %get-tuple-element.35.q_ref, f32[1,1024]{1,0:T(1,128)S(1)} %get-tuple-element.36.m_ref, f32[1,1024]{1,0:T(1,128)S(1)} %get-tuple-element.37.l_ref, ...), custom_call_target="tpu_custom_call" | custom-call | tf_op jit(solution)/shard_map/attend0/pallas_call | solution.py:297
  99.8 5.7 %collective-permute-start = (bf16[128,512]{1,0:T(8,128)(2,1)S(1)}, bf16[128,512]{1,0:T(8,128)(2,1)S(1)}, u32[]{:S(2)}, u32[]{:S(2)}) collective-permute-start(bf16[128,512]{1,0:T(8,128)(2,1)S(1)} %get-tuple-element.50), channel_id=1, source_target_pairs={{0,1},{1,0},{2,3},{3,2},{4,5},{5,4},{6,7},{7,6},{8,9},{9,8},{10,11... | collective-permute-start | bytes 393224 | tf_op jit(solution)/shard_map/ppermute | solution.py:475
  105.5 0.0 collective-permute-done.1.refs_1_.refs_3_
  105.5 1.0 collective-permute-done.b_ref
  106.5 5.4 %project4.1 = (bf16[32,5120]{1,0:T(8,128)(2,1)}, bf16[32,5120]{1,0:T(8,128)(2,1)S(1)}, bf16[32,5120]{1,0:T(8,128)(2,1)S(1)}, bf16[32,5120]{1,0:T(8,128)(2,1)S(1)}) custom-call(bf16[128,512]{1,0:T(8,128)(2,1)S(1)} %get-tuple-element.49.a_ref, bf16[128,512]{1,0:T(8,128)(2,1)S(1)} %collective-permute-done.b_ref, bf16[512,5120]{1,0:T(8,128)(2,1)} %refs_0_.3, ...), custom_call_target="tpu_custom_call" | custom-call | tf_op jit(solution)/shard_map/project4/pallas_call | solution.py:344
  111.8 3.1 %collective-permute-start.3 = (bf16[32,5120]{1,0:T(8,128)(2,1)}, bf16[32,5120]{1,0:T(8,128)(2,1)S(1)}, u32[]{:S(2)}, u32[]{:S(2)}) collective-permute-start(bf16[32,5120]{1,0:T(8,128)(2,1)} %get-tuple-element.51), channel_id=1, source_target_pairs={{0,2},{1,3},{2,4},{3,5},{4,6},{5,7},{6,0},{7,1},{8,10},{9,11},{10,... | collective-permute-start | bytes 983048 | tf_op jit(solution)/shard_map/ppermute | solution.py:480
  114.9 2.2 %collective-permute-start.4 = (bf16[32,5120]{1,0:T(8,128)(2,1)S(1)}, bf16[32,5120]{1,0:T(8,128)(2,1)S(1)}, u32[]{:S(2)}, u32[]{:S(2)}) collective-permute-start(bf16[32,5120]{1,0:T(8,128)(2,1)S(1)} %get-tuple-element.55), channel_id=1, source_target_pairs={{2,0},{3,1},{4,2},{5,3},{6,4},{7,5},{0,6},{1,7},{10,8},{11,9},{12,... | collective-permute-start | bytes 983048 | tf_op jit(solution)/shard_map/ppermute | solution.py:480
  117.1 8.3 %attend1.1 = (bf16[64,512]{1,0:T(8,128)(2,1)S(1)}, bf16[64,512]{1,0:T(8,128)(2,1)S(1)}) custom-call(s32[8,128]{1,0:T(8,128)S(1)} %copy-done.4, s32[1]{0:T(128)S(6)} %copy.17.length, bf16[512,128]{1,0:T(8,128)(2,1)S(1)} %get-tuple-element.39.q_ref, f32[1,512]{1,0:T(1,128)S(1)} %get-tuple-element.40.m_ref, f32[1,512]{1,0:T(1,128)S(1)} %get-tuple-element.41.l_ref, ...), custom_call_target="tpu_custom_call" | custom-call | tf_op jit(solution)/shard_map/attend1/pallas_call | solution.py:297
  125.5 0.7 collective-permute-start.2
  126.2 0.2 fusion.2
  126.4 2.6 %collective-permute-start.7 = (bf16[32,5120]{1,0:T(8,128)(2,1)S(1)}, bf16[32,5120]{1,0:T(8,128)(2,1)S(1)}, u32[]{:S(2)}, u32[]{:S(2)}) collective-permute-start(bf16[32,5120]{1,0:T(8,128)(2,1)S(1)} %get-tuple-element.62), channel_id=1, source_target_pairs={{2,0},{3,1},{4,2},{5,3},{6,4},{7,5},{0,6},{1,7},{10,8},{11,9},{12,... | collective-permute-start | bytes 983048 | tf_op jit(solution)/shard_map/ppermute | solution.py:481
  129.0 0.0 collective-permute-start.8
  129.0 0.0 collective-permute-done.2.b_ref
  129.0 2.2 %collective-permute-done.3.refs_0_ = bf16[32,5120]{1,0:T(8,128)(2,1)S(1)} collective-permute-done((bf16[32,5120]{1,0:T(8,128)(2,1)}, bf16[32,5120]{1,0:T(8,128)(2,1)S(1)}, u32[]{:S(2)}, u32[]{:S(2)}) %collective-permute-start.3) | collective-permute-done | bytes 327712 | tf_op jit(solution)/shard_map/ppermute | solution.py:480
  131.2 0.0 collective-permute-done.4.refs_1_
  131.2 4.5 %project2.2 = (bf16[32,5120]{1,0:T(8,128)(2,1)S(1)}, bf16[32,5120]{1,0:T(8,128)(2,1)S(1)}) custom-call(bf16[64,512]{1,0:T(8,128)(2,1)S(1)} %get-tuple-element.53.a_ref, bf16[64,512]{1,0:T(8,128)(2,1)S(1)} %collective-permute-done.2.b_ref, bf16[32,5120]{1,0:T(8,128)(2,1)S(1)} %collective-permute-done.3.refs_0_, ...), custom_call_target="tpu_custom_call" | custom-call | tf_op jit(solution)/shard_map/project2/pallas_call | solution.py:344
  135.8 2.2 %collective-permute-start.6 = (bf16[32,5120]{1,0:T(8,128)(2,1)S(1)}, bf16[32,5120]{1,0:T(8,128)(2,1)S(1)}, u32[]{:S(2)}, u32[]{:S(2)}) collective-permute-start(bf16[32,5120]{1,0:T(8,128)(2,1)S(1)} %get-tuple-element.56), channel_id=1, source_target_pairs={{0,2},{1,3},{2,4},{3,5},{4,6},{5,7},{6,0},{7,1},{8,10},{9,11},{10,... | collective-permute-start | bytes 983048 | tf_op jit(solution)/shard_map/ppermute | solution.py:483
  138.0 4.7 %collective-permute-start.9 = (bf16[32,5120]{1,0:T(8,128)(2,1)S(1)}, bf16[32,5120]{1,0:T(8,128)(2,1)S(1)}, u32[]{:S(2)}, u32[]{:S(2)}) collective-permute-start(bf16[32,5120]{1,0:T(8,128)(2,1)S(1)} %get-tuple-element.64), channel_id=1, source_target_pairs={{2,0},{3,1},{4,2},{5,3},{6,4},{7,5},{0,6},{1,7},{10,8},{11,9},{12,... | collective-permute-start | bytes 983048 | tf_op jit(solution)/shard_map/ppermute | solution.py:483
  142.6 0.1 fusion.slots
  142.7 8.3 %attend2.1 = (bf16[64,512]{1,0:T(8,128)(2,1)S(1)}, bf16[64,512]{1,0:T(8,128)(2,1)S(1)}) custom-call(s32[8,128]{1,0:T(8,128)S(1)} %copy-done.4, s32[1]{0:T(128)S(6)} %copy.17.length, bf16[512,128]{1,0:T(8,128)(2,1)S(1)} %get-tuple-element.43.q_ref, f32[1,512]{1,0:T(1,128)S(1)} %get-tuple-element.44.m_ref, f32[1,512]{1,0:T(1,128)S(1)} %get-tuple-element.45.l_ref, ...), custom_call_target="tpu_custom_call" | custom-call | tf_op jit(solution)/shard_map/attend2/pallas_call | solution.py:297
  151.1 5.3 %collective-permute-start.5 = (bf16[64,512]{1,0:T(8,128)(2,1)S(1)}, bf16[64,512]{1,0:T(8,128)(2,1)S(1)}, u32[]{:S(2)}, u32[]{:S(2)}) collective-permute-start(bf16[64,512]{1,0:T(8,128)(2,1)S(1)} %get-tuple-element.59), channel_id=1, source_target_pairs={{0,1},{1,0},{2,3},{3,2},{4,5},{5,4},{6,7},{7,6},{8,9},{9,8},{10,11... | collective-permute-start | bytes 196616 | tf_op jit(solution)/shard_map/ppermute | solution.py:475
  156.4 1.0 copy_bitcast_fusion
  157.4 0.0 collective-permute-done.5.b_ref
  157.4 4.5 %project2.3 = (bf16[32,5120]{1,0:T(8,128)(2,1)S(1)}, bf16[32,5120]{1,0:T(8,128)(2,1)S(1)}) custom-call(bf16[64,512]{1,0:T(8,128)(2,1)S(1)} %get-tuple-element.58.a_ref, bf16[64,512]{1,0:T(8,128)(2,1)S(1)} %collective-permute-done.5.b_ref, bf16[512,5120]{1,0:T(8,128)(2,1)} %refs_0_.3, bf16[512,5120]{1,0:T(8,128)(2,1)} %collective-permute-done.1.refs_1_.refs_3_), custom_call_target="tpu_custom_call" | custom-call | tf_op jit(solution)/shard_map/project2/pallas_call | solution.py:344
  162.0 1.8 %write.1 = bf16[32,256,128]{2,1,0:T(8,128)(2,1)} custom-call(s32[4]{0:T(128)S(1)} %fusion.slots, bf16[4,256,128]{2,1,0:T(8,128)(2,1)S(1)} %bitcast.28, bf16[32,256,128]{2,1,0:T(8,128)(2,1)} %copy_pool.1.kept_ref), custom_call_target="tpu_custom_call", output_to_operand_aliasing={{}: (2, {})} | custom-call | tf_op jit(solution)/shard_map/write/pallas_call | solution.py:409
  163.8 0.0 collective-permute-done.7.near_down
  163.8 0.0 collective-permute-done.8.near_up
  163.8 0.0 collective-permute-done.6.far_up
  163.9 0.0 collective-permute-done.9.far_down
  163.9 1.1 combine.1
  (2 shorter events, 0.0 us)
Async XLA Ops:
  3.9 15.1 %all-to-all-start = ((bf16[32,48,128]{2,1,0:T(8,128)(2,1)}), bf16[32,48,128]{2,1,0:T(8,128)(2,1)S(1)}, u32[]{:S(2)}, u32[]{:S(2)}) async-start(bf16[32,48,128]{2,1,0:T(8,128)(2,1)} %get-tuple-element.48), calls=%async_computation | async-start | bytes 786432 | tf_op jit(solution)/shard_map/all_to_all | solution.py:422
  12.2 1.6 copy-start
  22.6 9.8 %copy-start.1 = (bf16[32,128,2,128]{3,2,1,0:T(2,128)(2,1)S(1)}, bf16[32,128,2,128]{3,2,1,0:T(2,128)(2,1)}, u32[]{:S(2)}) copy-start(bf16[32,128,2,128]{3,2,1,0:T(2,128)(2,1)} %param.12) | copy-start | bytes 6291460
  22.6 11.4 %copy-start.2 = (bf16[512,2,128]{2,1,0:T(2,128)(2,1)S(1)}, bf16[512,2,128]{2,1,0:T(2,128)(2,1)}, u32[]{:S(2)}) copy-start(bf16[512,2,128]{2,1,0:T(2,128)(2,1)} %param.11) | copy-start | bytes 786436
  22.6 61.7 %all-to-all-start.1 = ((bf16[32,544,128]{2,1,0:T(8,128)(2,1)}), bf16[32,544,128]{2,1,0:T(8,128)(2,1)}, u32[]{:S(2)}, u32[]{:S(2)}) async-start(bf16[32,544,128]{2,1,0:T(8,128)(2,1)} %gather.1), calls=%async_computation.1 | async-start | bytes 8912896 | tf_op jit(solution)/shard_map/all_to_all | solution.py:422
  29.4 5.1 %copy-start.3 = (bf16[512,512]{1,0:T(8,128)(2,1)S(1)}, bf16[512,512]{1,0:T(8,128)(2,1)}, u32[]{:S(2)}) copy-start(bf16[512,512]{1,0:T(8,128)(2,1)} %q_ref.1) | copy-start | bytes 1572868
  29.5 54.9 %copy-start.4 = (s32[8,128]{1,0:T(8,128)S(1)}, s32[8,128]{1,0:T(8,128)}, u32[]{:S(2)}) copy-start(s32[8,128]{1,0:T(8,128)} %get-tuple-element.57.blocks) | copy-start | bytes 12292
  29.5 76.0 %collective-permute-start.1 = (bf16[512,5120]{1,0:T(8,128)(2,1)}, bf16[512,5120]{1,0:T(8,128)(2,1)}, u32[]{:S(2)}, u32[]{:S(2)}) collective-permute-start(bf16[512,5120]{1,0:T(8,128)(2,1)} %refs_0_.3), channel_id=1, source_target_pairs={{0,1},{1,0},{2,3},{3,2},{4,5},{5,4},{6,7},{7,6},{8,9},{9,8},{10,11... | collective-permute-start | bytes 15728648 | tf_op jit(solution)/shard_map/ppermute | solution.py:467
  99.8 6.7 %collective-permute-start = (bf16[128,512]{1,0:T(8,128)(2,1)S(1)}, bf16[128,512]{1,0:T(8,128)(2,1)S(1)}, u32[]{:S(2)}, u32[]{:S(2)}) collective-permute-start(bf16[128,512]{1,0:T(8,128)(2,1)S(1)} %get-tuple-element.50), channel_id=1, source_target_pairs={{0,1},{1,0},{2,3},{3,2},{4,5},{5,4},{6,7},{7,6},{8,9},{9,8},{10,11... | collective-permute-start | bytes 393224 | tf_op jit(solution)/shard_map/ppermute | solution.py:475
  111.8 19.4 %collective-permute-start.3 = (bf16[32,5120]{1,0:T(8,128)(2,1)}, bf16[32,5120]{1,0:T(8,128)(2,1)S(1)}, u32[]{:S(2)}, u32[]{:S(2)}) collective-permute-start(bf16[32,5120]{1,0:T(8,128)(2,1)} %get-tuple-element.51), channel_id=1, source_target_pairs={{0,2},{1,3},{2,4},{3,5},{4,6},{5,7},{6,0},{7,1},{8,10},{9,11},{10,... | collective-permute-start | bytes 983048 | tf_op jit(solution)/shard_map/ppermute | solution.py:480
  114.9 16.3 %collective-permute-start.4 = (bf16[32,5120]{1,0:T(8,128)(2,1)S(1)}, bf16[32,5120]{1,0:T(8,128)(2,1)S(1)}, u32[]{:S(2)}, u32[]{:S(2)}) collective-permute-start(bf16[32,5120]{1,0:T(8,128)(2,1)S(1)} %get-tuple-element.55), channel_id=1, source_target_pairs={{2,0},{3,1},{4,2},{5,3},{6,4},{7,5},{0,6},{1,7},{10,8},{11,9},{12,... | collective-permute-start | bytes 983048 | tf_op jit(solution)/shard_map/ppermute | solution.py:480
  125.5 3.5 %collective-permute-start.2 = (bf16[64,512]{1,0:T(8,128)(2,1)S(1)}, bf16[64,512]{1,0:T(8,128)(2,1)S(1)}, u32[]{:S(2)}, u32[]{:S(2)}) collective-permute-start(bf16[64,512]{1,0:T(8,128)(2,1)S(1)} %get-tuple-element.54), channel_id=1, source_target_pairs={{0,1},{1,0},{2,3},{3,2},{4,5},{5,4},{6,7},{7,6},{8,9},{9,8},{10,11... | collective-permute-start | bytes 196616 | tf_op jit(solution)/shard_map/ppermute | solution.py:475
  126.4 37.4 %collective-permute-start.7 = (bf16[32,5120]{1,0:T(8,128)(2,1)S(1)}, bf16[32,5120]{1,0:T(8,128)(2,1)S(1)}, u32[]{:S(2)}, u32[]{:S(2)}) collective-permute-start(bf16[32,5120]{1,0:T(8,128)(2,1)S(1)} %get-tuple-element.62), channel_id=1, source_target_pairs={{2,0},{3,1},{4,2},{5,3},{6,4},{7,5},{0,6},{1,7},{10,8},{11,9},{12,... | collective-permute-start | bytes 983048 | tf_op jit(solution)/shard_map/ppermute | solution.py:481
  129.0 34.8 %collective-permute-start.8 = (bf16[32,5120]{1,0:T(8,128)(2,1)S(1)}, bf16[32,5120]{1,0:T(8,128)(2,1)S(1)}, u32[]{:S(2)}, u32[]{:S(2)}) collective-permute-start(bf16[32,5120]{1,0:T(8,128)(2,1)S(1)} %get-tuple-element.63), channel_id=1, source_target_pairs={{0,2},{1,3},{2,4},{3,5},{4,6},{5,7},{6,0},{7,1},{8,10},{9,11},{10,... | collective-permute-start | bytes 983048 | tf_op jit(solution)/shard_map/ppermute | solution.py:481
  135.8 28.1 %collective-permute-start.6 = (bf16[32,5120]{1,0:T(8,128)(2,1)S(1)}, bf16[32,5120]{1,0:T(8,128)(2,1)S(1)}, u32[]{:S(2)}, u32[]{:S(2)}) collective-permute-start(bf16[32,5120]{1,0:T(8,128)(2,1)S(1)} %get-tuple-element.56), channel_id=1, source_target_pairs={{0,2},{1,3},{2,4},{3,5},{4,6},{5,7},{6,0},{7,1},{8,10},{9,11},{10,... | collective-permute-start | bytes 983048 | tf_op jit(solution)/shard_map/ppermute | solution.py:483
  138.0 25.9 %collective-permute-start.9 = (bf16[32,5120]{1,0:T(8,128)(2,1)S(1)}, bf16[32,5120]{1,0:T(8,128)(2,1)S(1)}, u32[]{:S(2)}, u32[]{:S(2)}) collective-permute-start(bf16[32,5120]{1,0:T(8,128)(2,1)S(1)} %get-tuple-element.64), channel_id=1, source_target_pairs={{2,0},{3,1},{4,2},{5,3},{6,4},{7,5},{0,6},{1,7},{10,8},{11,9},{12,... | collective-permute-start | bytes 983048 | tf_op jit(solution)/shard_map/ppermute | solution.py:483
  151.1 6.4 %collective-permute-start.5 = (bf16[64,512]{1,0:T(8,128)(2,1)S(1)}, bf16[64,512]{1,0:T(8,128)(2,1)S(1)}, u32[]{:S(2)}, u32[]{:S(2)}) collective-permute-start(bf16[64,512]{1,0:T(8,128)(2,1)S(1)} %get-tuple-element.59), channel_id=1, source_target_pairs={{0,1},{1,0},{2,3},{3,2},{4,5},{5,4},{6,7},{7,6},{8,9},{9,8},{10,11... | collective-permute-start | bytes 196616 | tf_op jit(solution)/shard_map/ppermute | solution.py:475
where the time goes:
time: 166 us; the launch traced here: 165 us
  Pallas kernels  60.9 us (37%)
  waiting for transfers between devices  54.1 us (33%)
  starting transfers between devices  44.6 us (27%)
  local copies, waits for them, and re-layouts  2.72 us (2%)
  between operations  2.27 us (1%)
    all_to_all x2, waiting for transfers between devices, swap_pool(): return lax.all_to_all(x, 'pool', split_axis=0, concat_axis=0, tiled=True)  50.9 us
    pallas_call x3, Pallas kernels, attend(): pl.pallas_call(attend_kernel, out_shape=(out, out), in_specs=[SMEM, SMEM,...  32.1 us
    all_to_all x2, starting transfers between devices, swap_pool(): return lax.all_to_all(x, 'pool', split_axis=0, concat_axis=0, tiled=True)  15.1 us
    pallas_call x3, Pallas kernels, project(): pl.pallas_call(functools.partial(project_kernel, arriving=len(arrived)),...  14.4 us
    ppermute x3, starting transfers between devices, contexts(): return (mine, swap(theirs))  11.8 us
    ppermute x2, starting transfers between devices, on_device(): far_up, far_down = (send_up(up), send_down(down))  6.87 us
    ppermute x2, starting transfers between devices, on_device(): through_up, through_down = (send_up(up), send_down(down))  5.29 us
    pallas_call x1, Pallas kernels, gather_blocks(): pl.pallas_call(gather_kernel, out_shape=jax.ShapeDtypeStruct((pool, 512 +...  3.55 us
  transfers between devices with their start and end apart: 12, of which 4 were waited for; matrix products, arithmetic and copies ran while one was open for 1% of the time, Pallas kernels for 30%

commit v1 on v0

--- a/solution.py
+++ b/solution.py
@@ -469,9 +469,10 @@
 
     heads = queries.shape[1] // HEAD
 
-    def contexts(group, after):
+    def contexts(group, after, before_swap=()):
         used, _ = lax.optimization_barrier((blocks, after))
         mine, theirs = attend(starts[group], kv, used, hist_len, heads, group)
+        theirs, _ = lax.optimization_barrier((theirs, before_swap))
         return mine, swap(theirs)
 
     up, down, near_up, near_down = project(
@@ -485,7 +486,7 @@
     returned = kv[:, 512:].reshape(pool, 4, 8, 128).transpose(1, 0, 2, 3)
     mine = (told[:, 2:6] == me) & (told[:, 10:11] > 0)
     slots = jnp.max(jnp.where(mine, told[:, 6:10], -1), axis=0)
-    top, bottom = project(*contexts(2, up), out_weight, other_weight)
+    top, bottom = project(*contexts(2, up, (near_up, near_down)), out_weight, other_weight)
     returned, _ = lax.optimization_barrier((returned, top))
     pool_out = write_back(slots, returned.reshape(4, 256, 128), kept).reshape(saved.shape)
     attn_out = combine(top, bottom, far_up, near_down, near_up, far_down)

time: 166 us -> 167 us (level)
  the two profiles are of different devices: /device:TPU:13 before, /device:TPU:1 now
where the time goes in v1:
time: 167 us
  waiting for transfers between devices  66.7 us (40%)
  Pallas kernels  58.8 us (35%)
  starting transfers between devices  36 us (22%)
  local copies, waits for them, and re-layouts  2.72 us (2%)
  between operations  2.27 us (1%)
    all_to_all x2, waiting for transfers between devices, swap_pool(): return lax.all_to_all(x, 'pool', split_axis=0, concat_axis=0, tiled=True)  56.6 us
    pallas_call x3, Pallas kernels, attend(): pl.pallas_call(attend_kernel, out_shape=(out, out), in_specs=[SMEM, SMEM,...  30.5 us
    pallas_call x3, Pallas kernels, project(): pl.pallas_call(functools.partial(project_kernel, arriving=len(arrived)),...  14.5 us
    all_to_all x2, starting transfers between devices, swap_pool(): return lax.all_to_all(x, 'pool', split_axis=0, concat_axis=0, tiled=True)  14.2 us
    ppermute x2, waiting for transfers between devices, on_device(): through_up, through_down = (send_up(up), send_down(down))  8.34 us
    ppermute x3, starting transfers between devices, contexts(): return (mine, swap(theirs))  6.53 us
    ppermute x2, starting transfers between devices, on_device(): through_up, through_down = (send_up(up), send_down(down))  5.29 us
    ppermute x2, starting transfers between devices, on_device(): far_up, far_down = (send_up(up), send_down(down))  3.65 us
  transfers between devices with their start and end apart: 12, of which 5 were waited for; matrix products, arithmetic and copies ran while one was open for 1% of the time, Pallas kernels for 28%

profile of v1, /device:TPU:1, one launch (start us, length us, event | category | flops | bytes accessed | tf_op | source)
XLA Modules:
  0.0 166.7 jit_solution(12634402007333528763)
XLA Ops:
  1.9 2.0 %table.1 = (bf16[32,48,128]{2,1,0:T(8,128)(2,1)}, s32[8,128]{1,0:T(8,128)}) custom-call(s32[1]{0:T(128)S(6)} %copy.17.length, s32[1,4]{1,0:T(1,128)} %dest_owner.1, s32[1,4]{1,0:T(1,128)} %dest_slot.1, s32[1]{0:T(128)S(6)} %copy.18.evict, s32[1,64]{1,0:T(1,128)} %owner_ref.1, s32[1,64]{1,0:T(1,128)} %block_ref.1, bf16[4,256,128]{2,1,0:T(8,128)(2,1)} %bitcast.29), custom_call_target="tpu_custom_call" | custom-call | tf_op jit(solution)/shard_map/table/pallas_call | solution.py:73
  3.9 9.2 %all-to-all-start = ((bf16[32,48,128]{2,1,0:T(8,128)(2,1)}), bf16[32,48,128]{2,1,0:T(8,128)(2,1)S(1)}, u32[]{:S(2)}, u32[]{:S(2)}) async-start(bf16[32,48,128]{2,1,0:T(8,128)(2,1)} %get-tuple-element.49), calls=%async_computation | async-start | bytes 786432 | tf_op jit(solution)/shard_map/all_to_all | solution.py:422
  13.2 0.0 copy-start
  13.2 1.6 copy-done
  14.8 1.3 split32.1.pool_ref
  16.1 5.7 %all-to-all-done = bf16[32,48,128]{2,1,0:T(8,128)(2,1)S(1)} async-done(((bf16[32,48,128]{2,1,0:T(8,128)(2,1)}), bf16[32,48,128]{2,1,0:T(8,128)(2,1)S(1)}, u32[]{:S(2)}, u32[]{:S(2)}) %all-to-all-start) | async-done | bytes 393248 | tf_op jit(solution)/shard_map/all_to_all | solution.py:422
  21.9 3.5 %gather.1 = bf16[32,544,128]{2,1,0:T(8,128)(2,1)} custom-call(s32[32,128]{1,0:T(8,128)S(1)} %bitcast.31, bf16[32,256,128]{2,1,0:T(8,128)(2,1)S(1)} %split32.1.pool_ref, bf16[32,32,128]{2,1,0:T(8,128)(2,1)S(1)} %slice.25.held_ref), custom_call_target="tpu_custom_call" | custom-call | tf_op jit(solution)/shard_map/gather/pallas_call | solution.py:137
  25.4 0.0 copy-start.1
  25.4 0.0 copy-start.2
  25.4 5.0 %all-to-all-start.1 = ((bf16[32,544,128]{2,1,0:T(8,128)(2,1)}), bf16[32,544,128]{2,1,0:T(8,128)(2,1)}, u32[]{:S(2)}, u32[]{:S(2)}) async-start(bf16[32,544,128]{2,1,0:T(8,128)(2,1)} %gather.1), calls=%async_computation.1 | async-start | bytes 8912896 | tf_op jit(solution)/shard_map/all_to_all | solution.py:422
  30.5 0.0 copy-start.3
  30.5 0.0 copy-start.4
  30.5 2.7 %collective-permute-start.1 = (bf16[512,5120]{1,0:T(8,128)(2,1)}, bf16[512,5120]{1,0:T(8,128)(2,1)}, u32[]{:S(2)}, u32[]{:S(2)}) collective-permute-start(bf16[512,5120]{1,0:T(8,128)(2,1)} %refs_0_.3), channel_id=1, source_target_pairs={{0,1},{1,0},{2,3},{3,2},{4,5},{5,4},{6,7},{7,6},{8,9},{9,8},{10,11... | collective-permute-start | bytes 15728648 | tf_op jit(solution)/shard_map/ppermute | solution.py:467
  33.2 0.0 copy-done.1
  33.2 1.5 copy_pool.1.kept_ref
  34.7 0.0 copy-done.2
  34.8 0.3 split4.1.new_ref
  35.1 0.1 stack.67.base
  35.2 0.0 copy-done.3
  35.2 2.8 %begin.1 = (bf16[1024,128]{1,0:T(8,128)(2,1)S(1)}, f32[1,1024]{1,0:T(1,128)S(1)}, f32[1,1024]{1,0:T(1,128)S(1)}, f32[128,1024]{1,0:T(8,128)S(1)}, bf16[512,128]{...) custom-call(s32[16]{0:T(128)S(1)} %stack.67.base, ...), custom_call_target="tpu_custom_call" | custom-call | tf_op jit(solution)/shard_map/begin/pallas_call | solution.py:207
  38.1 50.9 %all-to-all-done.1.kv_any = bf16[32,544,128]{2,1,0:T(8,128)(2,1)} async-done(((bf16[32,544,128]{2,1,0:T(8,128)(2,1)}), bf16[32,544,128]{2,1,0:T(8,128)(2,1)}, u32[]{:S(2)}, u32[]{:S(2)}) %all-to-all-start.1) | async-done | bytes 4456480 | tf_op jit(solution)/shard_map/all_to_all | solution.py:422
  88.9 0.0 copy-done.4
  88.9 14.4 %attend0.1 = (bf16[128,512]{1,0:T(8,128)(2,1)S(1)}, bf16[128,512]{1,0:T(8,128)(2,1)S(1)}) custom-call(s32[8,128]{1,0:T(8,128)S(1)} %copy-done.4, s32[1]{0:T(128)S(6)} %copy.17.length, bf16[1024,128]{1,0:T(8,128)(2,1)S(1)} %get-tuple-element.36.q_ref, f32[1,1024]{1,0:T(1,128)S(1)} %get-tuple-element.37.m_ref, f32[1,1024]{1,0:T(1,128)S(1)} %get-tuple-element.38.l_ref, ...), custom_call_target="tpu_custom_call" | custom-call | tf_op jit(solution)/shard_map/attend0/pallas_call | solution.py:297
  103.4 3.9 %collective-permute-start = (bf16[128,512]{1,0:T(8,128)(2,1)S(1)}, bf16[128,512]{1,0:T(8,128)(2,1)S(1)}, u32[]{:S(2)}, u32[]{:S(2)}) collective-permute-start(bf16[128,512]{1,0:T(8,128)(2,1)S(1)} %get-tuple-element.51), channel_id=1, source_target_pairs={{0,1},{1,0},{2,3},{3,2},{4,5},{5,4},{6,7},{7,6},{8,9},{9,8},{10,11... | collective-permute-start | bytes 393224 | tf_op jit(solution)/shard_map/ppermute | solution.py:476
  107.2 0.0 collective-permute-done.1.refs_1_.refs_3_
  107.2 1.0 collective-permute-done.b_ref
  108.2 5.5 %project4.1 = (bf16[32,5120]{1,0:T(8,128)(2,1)}, bf16[32,5120]{1,0:T(8,128)(2,1)}, bf16[32,5120]{1,0:T(8,128)(2,1)S(1)}, bf16[32,5120]{1,0:T(8,128)(2,1)S(1)}) custom-call(bf16[128,512]{1,0:T(8,128)(2,1)S(1)} %get-tuple-element.50.a_ref, bf16[128,512]{1,0:T(8,128)(2,1)S(1)} %collective-permute-done.b_ref, bf16[512,5120]{1,0:T(8,128)(2,1)} %refs_0_.3, ...), custom_call_target="tpu_custom_call" | custom-call | tf_op jit(solution)/shard_map/project4/pallas_call | solution.py:344
  113.7 3.1 %collective-permute-start.3 = (bf16[32,5120]{1,0:T(8,128)(2,1)}, bf16[32,5120]{1,0:T(8,128)(2,1)S(1)}, u32[]{:S(2)}, u32[]{:S(2)}) collective-permute-start(bf16[32,5120]{1,0:T(8,128)(2,1)} %get-tuple-element.52), channel_id=1, source_target_pairs={{0,2},{1,3},{2,4},{3,5},{4,6},{5,7},{6,0},{7,1},{8,10},{9,11},{10,... | collective-permute-start | bytes 983048 | tf_op jit(solution)/shard_map/ppermute | solution.py:481
  116.8 2.2 %collective-permute-start.4 = (bf16[32,5120]{1,0:T(8,128)(2,1)}, bf16[32,5120]{1,0:T(8,128)(2,1)S(1)}, u32[]{:S(2)}, u32[]{:S(2)}) collective-permute-start(bf16[32,5120]{1,0:T(8,128)(2,1)} %get-tuple-element.56), channel_id=1, source_target_pairs={{2,0},{3,1},{4,2},{5,3},{6,4},{7,5},{0,6},{1,7},{10,8},{11,9},{12,... | collective-permute-start | bytes 983048 | tf_op jit(solution)/shard_map/ppermute | solution.py:481
  119.0 1.1 collective-permute-start.5
  120.1 2.5 %collective-permute-start.6 = (bf16[32,5120]{1,0:T(8,128)(2,1)S(1)}, bf16[32,5120]{1,0:T(8,128)(2,1)S(1)}, u32[]{:S(2)}, u32[]{:S(2)}) collective-permute-start(bf16[32,5120]{1,0:T(8,128)(2,1)S(1)} %get-tuple-element.62), channel_id=1, source_target_pairs={{2,0},{3,1},{4,2},{5,3},{6,4},{7,5},{0,6},{1,7},{10,8},{11,9},{12,... | collective-permute-start | bytes 983048 | tf_op jit(solution)/shard_map/ppermute | solution.py:482
  122.6 8.0 %attend1.1 = (bf16[64,512]{1,0:T(8,128)(2,1)S(1)}, bf16[64,512]{1,0:T(8,128)(2,1)S(1)}) custom-call(s32[8,128]{1,0:T(8,128)S(1)} %copy-done.4, s32[1]{0:T(128)S(6)} %copy.17.length, bf16[512,128]{1,0:T(8,128)(2,1)S(1)} %get-tuple-element.40.q_ref, f32[1,512]{1,0:T(1,128)S(1)} %get-tuple-element.41.m_ref, f32[1,512]{1,0:T(1,128)S(1)} %get-tuple-element.42.l_ref, ...), custom_call_target="tpu_custom_call" | custom-call | tf_op jit(solution)/shard_map/attend1/pallas_call | solution.py:297
  130.6 1.5 collective-permute-start.2
  132.1 0.2 fusion.2
  132.3 0.7 collective-permute-done.2.b_ref
  133.0 8.3 %collective-permute-done.3.refs_0_ = bf16[32,5120]{1,0:T(8,128)(2,1)S(1)} collective-permute-done((bf16[32,5120]{1,0:T(8,128)(2,1)}, bf16[32,5120]{1,0:T(8,128)(2,1)S(1)}, u32[]{:S(2)}, u32[]{:S(2)}) %collective-permute-start.3) | collective-permute-done | bytes 327712 | tf_op jit(solution)/shard_map/ppermute | solution.py:481
  141.3 0.0 collective-permute-done.4.refs_1_
  141.3 4.5 %project2.2 = (bf16[32,5120]{1,0:T(8,128)(2,1)S(1)}, bf16[32,5120]{1,0:T(8,128)(2,1)S(1)}) custom-call(bf16[64,512]{1,0:T(8,128)(2,1)S(1)} %get-tuple-element.54.a_ref, bf16[64,512]{1,0:T(8,128)(2,1)S(1)} %collective-permute-done.2.b_ref, bf16[32,5120]{1,0:T(8,128)(2,1)S(1)} %collective-permute-done.3.refs_0_, ...), custom_call_target="tpu_custom_call" | custom-call | tf_op jit(solution)/shard_map/project2/pallas_call | solution.py:344
  145.9 3.4 %collective-permute-start.8 = (bf16[32,5120]{1,0:T(8,128)(2,1)S(1)}, bf16[32,5120]{1,0:T(8,128)(2,1)S(1)}, u32[]{:S(2)}, u32[]{:S(2)}) collective-permute-start(bf16[32,5120]{1,0:T(8,128)(2,1)S(1)} %get-tuple-element.57), channel_id=1, source_target_pairs={{0,2},{1,3},{2,4},{3,5},{4,6},{5,7},{6,0},{7,1},{8,10},{9,11},{10,... | collective-permute-start | bytes 983048 | tf_op jit(solution)/shard_map/ppermute | solution.py:484
  149.3 0.2 collective-permute-start.9
  149.5 0.1 fusion.slots
  149.6 8.0 %attend2.1 = (bf16[64,512]{1,0:T(8,128)(2,1)S(1)}, bf16[64,512]{1,0:T(8,128)(2,1)S(1)}) custom-call(s32[8,128]{1,0:T(8,128)S(1)} %copy-done.4, s32[1]{0:T(128)S(6)} %copy.17.length, bf16[512,128]{1,0:T(8,128)(2,1)S(1)} %get-tuple-element.44.q_ref, f32[1,512]{1,0:T(1,128)S(1)} %get-tuple-element.45.m_ref, f32[1,512]{1,0:T(1,128)S(1)} %get-tuple-element.46.l_ref, ...), custom_call_target="tpu_custom_call" | custom-call | tf_op jit(solution)/shard_map/attend2/pallas_call | solution.py:297
  157.7 0.0 collective-permute-done.5.near_up
  157.7 0.0 collective-permute-done.6.near_down
  157.7 1.2 collective-permute-start.7
  158.9 1.0 copy_bitcast_fusion
  159.9 0.0 collective-permute-done.7.b_ref
  159.9 4.5 %project2.3 = (bf16[32,5120]{1,0:T(8,128)(2,1)S(1)}, bf16[32,5120]{1,0:T(8,128)(2,1)S(1)}) custom-call(bf16[64,512]{1,0:T(8,128)(2,1)S(1)} %get-tuple-element.59.a_ref, bf16[64,512]{1,0:T(8,128)(2,1)S(1)} %collective-permute-done.7.b_ref, bf16[512,5120]{1,0:T(8,128)(2,1)} %refs_0_.3, bf16[512,5120]{1,0:T(8,128)(2,1)} %collective-permute-done.1.refs_1_.refs_3_), custom_call_target="tpu_custom_call" | custom-call | tf_op jit(solution)/shard_map/project2/pallas_call | solution.py:344
  164.4 1.2 write.1
  165.6 0.0 collective-permute-done.8.far_up
  165.6 0.0 collective-permute-done.9.far_down
  165.7 1.1 combine.1
  (2 shorter events, 0.0 us)
Async XLA Ops:
  3.9 17.9 %all-to-all-start = ((bf16[32,48,128]{2,1,0:T(8,128)(2,1)}), bf16[32,48,128]{2,1,0:T(8,128)(2,1)S(1)}, u32[]{:S(2)}, u32[]{:S(2)}) async-start(bf16[32,48,128]{2,1,0:T(8,128)(2,1)} %get-tuple-element.49), calls=%async_computation | async-start | bytes 786432 | tf_op jit(solution)/shard_map/all_to_all | solution.py:422
  13.2 1.6 copy-start
  25.4 7.8 %copy-start.1 = (bf16[32,128,2,128]{3,2,1,0:T(2,128)(2,1)S(1)}, bf16[32,128,2,128]{3,2,1,0:T(2,128)(2,1)}, u32[]{:S(2)}) copy-start(bf16[32,128,2,128]{3,2,1,0:T(2,128)(2,1)} %param.12) | copy-start | bytes 6291460
  25.4 9.3 %copy-start.2 = (bf16[512,2,128]{2,1,0:T(2,128)(2,1)S(1)}, bf16[512,2,128]{2,1,0:T(2,128)(2,1)}, u32[]{:S(2)}) copy-start(bf16[512,2,128]{2,1,0:T(2,128)(2,1)} %param.11) | copy-start | bytes 786436
  25.4 63.5 %all-to-all-start.1 = ((bf16[32,544,128]{2,1,0:T(8,128)(2,1)}), bf16[32,544,128]{2,1,0:T(8,128)(2,1)}, u32[]{:S(2)}, u32[]{:S(2)}) async-start(bf16[32,544,128]{2,1,0:T(8,128)(2,1)} %gather.1), calls=%async_computation.1 | async-start | bytes 8912896 | tf_op jit(solution)/shard_map/all_to_all | solution.py:422
  30.5 4.8 %copy-start.3 = (bf16[512,512]{1,0:T(8,128)(2,1)S(1)}, bf16[512,512]{1,0:T(8,128)(2,1)}, u32[]{:S(2)}) copy-start(bf16[512,512]{1,0:T(8,128)(2,1)} %q_ref.1) | copy-start | bytes 1572868
  30.5 58.5 %copy-start.4 = (s32[8,128]{1,0:T(8,128)S(1)}, s32[8,128]{1,0:T(8,128)}, u32[]{:S(2)}) copy-start(s32[8,128]{1,0:T(8,128)} %get-tuple-element.58.blocks) | copy-start | bytes 12292
  30.5 76.7 %collective-permute-start.1 = (bf16[512,5120]{1,0:T(8,128)(2,1)}, bf16[512,5120]{1,0:T(8,128)(2,1)}, u32[]{:S(2)}, u32[]{:S(2)}) collective-permute-start(bf16[512,5120]{1,0:T(8,128)(2,1)} %refs_0_.3), channel_id=1, source_target_pairs={{0,1},{1,0},{2,3},{3,2},{4,5},{5,4},{6,7},{7,6},{8,9},{9,8},{10,11... | collective-permute-start | bytes 15728648 | tf_op jit(solution)/shard_map/ppermute | solution.py:467
  103.4 4.8 %collective-permute-start = (bf16[128,512]{1,0:T(8,128)(2,1)S(1)}, bf16[128,512]{1,0:T(8,128)(2,1)S(1)}, u32[]{:S(2)}, u32[]{:S(2)}) collective-permute-start(bf16[128,512]{1,0:T(8,128)(2,1)S(1)} %get-tuple-element.51), channel_id=1, source_target_pairs={{0,1},{1,0},{2,3},{3,2},{4,5},{5,4},{6,7},{7,6},{8,9},{9,8},{10,11... | collective-permute-start | bytes 393224 | tf_op jit(solution)/shard_map/ppermute | solution.py:476
  113.7 27.6 %collective-permute-start.3 = (bf16[32,5120]{1,0:T(8,128)(2,1)}, bf16[32,5120]{1,0:T(8,128)(2,1)S(1)}, u32[]{:S(2)}, u32[]{:S(2)}) collective-permute-start(bf16[32,5120]{1,0:T(8,128)(2,1)} %get-tuple-element.52), channel_id=1, source_target_pairs={{0,2},{1,3},{2,4},{3,5},{4,6},{5,7},{6,0},{7,1},{8,10},{9,11},{10,... | collective-permute-start | bytes 983048 | tf_op jit(solution)/shard_map/ppermute | solution.py:481
  116.8 24.6 %collective-permute-start.4 = (bf16[32,5120]{1,0:T(8,128)(2,1)}, bf16[32,5120]{1,0:T(8,128)(2,1)S(1)}, u32[]{:S(2)}, u32[]{:S(2)}) collective-permute-start(bf16[32,5120]{1,0:T(8,128)(2,1)} %get-tuple-element.56), channel_id=1, source_target_pairs={{2,0},{3,1},{4,2},{5,3},{6,4},{7,5},{0,6},{1,7},{10,8},{11,9},{12,... | collective-permute-start | bytes 983048 | tf_op jit(solution)/shard_map/ppermute | solution.py:481
  119.0 38.7 %collective-permute-start.5 = (bf16[32,5120]{1,0:T(8,128)(2,1)S(1)}, bf16[32,5120]{1,0:T(8,128)(2,1)S(1)}, u32[]{:S(2)}, u32[]{:S(2)}) collective-permute-start(bf16[32,5120]{1,0:T(8,128)(2,1)S(1)} %get-tuple-element.61), channel_id=1, source_target_pairs={{0,2},{1,3},{2,4},{3,5},{4,6},{5,7},{6,0},{7,1},{8,10},{9,11},{10,... | collective-permute-start | bytes 983048 | tf_op jit(solution)/shard_map/ppermute | solution.py:482
  120.1 37.6 %collective-permute-start.6 = (bf16[32,5120]{1,0:T(8,128)(2,1)S(1)}, bf16[32,5120]{1,0:T(8,128)(2,1)S(1)}, u32[]{:S(2)}, u32[]{:S(2)}) collective-permute-start(bf16[32,5120]{1,0:T(8,128)(2,1)S(1)} %get-tuple-element.62), channel_id=1, source_target_pairs={{2,0},{3,1},{4,2},{5,3},{6,4},{7,5},{0,6},{1,7},{10,8},{11,9},{12,... | collective-permute-start | bytes 983048 | tf_op jit(solution)/shard_map/ppermute | solution.py:482
  130.6 2.4 %collective-permute-start.2 = (bf16[64,512]{1,0:T(8,128)(2,1)S(1)}, bf16[64,512]{1,0:T(8,128)(2,1)S(1)}, u32[]{:S(2)}, u32[]{:S(2)}) collective-permute-start(bf16[64,512]{1,0:T(8,128)(2,1)S(1)} %get-tuple-element.55), channel_id=1, source_target_pairs={{0,1},{1,0},{2,3},{3,2},{4,5},{5,4},{6,7},{7,6},{8,9},{9,8},{10,11... | collective-permute-start | bytes 196616 | tf_op jit(solution)/shard_map/ppermute | solution.py:476
  145.9 19.8 %collective-permute-start.8 = (bf16[32,5120]{1,0:T(8,128)(2,1)S(1)}, bf16[32,5120]{1,0:T(8,128)(2,1)S(1)}, u32[]{:S(2)}, u32[]{:S(2)}) collective-permute-start(bf16[32,5120]{1,0:T(8,128)(2,1)S(1)} %get-tuple-element.57), channel_id=1, source_target_pairs={{0,2},{1,3},{2,4},{3,5},{4,6},{5,7},{6,0},{7,1},{8,10},{9,11},{10,... | collective-permute-start | bytes 983048 | tf_op jit(solution)/shard_map/ppermute | solution.py:484
  149.3 16.3 %collective-permute-start.9 = (bf16[32,5120]{1,0:T(8,128)(2,1)S(1)}, bf16[32,5120]{1,0:T(8,128)(2,1)S(1)}, u32[]{:S(2)}, u32[]{:S(2)}) collective-permute-start(bf16[32,5120]{1,0:T(8,128)(2,1)S(1)} %get-tuple-element.66), channel_id=1, source_target_pairs={{2,0},{3,1},{4,2},{5,3},{6,4},{7,5},{0,6},{1,7},{10,8},{11,9},{12,... | collective-permute-start | bytes 983048 | tf_op jit(solution)/shard_map/ppermute | solution.py:484
  157.7 2.2 %collective-permute-start.7 = (bf16[64,512]{1,0:T(8,128)(2,1)S(1)}, bf16[64,512]{1,0:T(8,128)(2,1)S(1)}, u32[]{:S(2)}, u32[]{:S(2)}) collective-permute-start(bf16[64,512]{1,0:T(8,128)(2,1)S(1)} %get-tuple-element.63), channel_id=1, source_target_pairs={{0,1},{1,0},{2,3},{3,2},{4,5},{5,4},{6,7},{7,6},{8,9},{9,8},{10,11... | collective-permute-start | bytes 196616 | tf_op jit(solution)/shard_map/ppermute | solution.py:476
